TPU v7x, 32 devices: a whole 2x2x4 slice. The times are simulated.
32 devices in a mesh: group: 2 (over y), section: 4 (over z), dp: 4 (over x, core).
Axes of the slice: x: 2, y: 2, z: 4, core: 2. Of those that a mesh axis runs over, the one named last changes fastest.
Arguments:
- tokens: bfloat16 [4, 8, 32, 1600], P(None, ('group', 'dp')), parts along dimension 1, may hold values from -6 to 6
- pixel_index: int32 [4, 8, 384], P(None, ('group', 'dp')), parts along dimension 1, may hold values from 0 to 6271
- point_mask: int32 [4, 8, 384], P(None, ('group', 'dp')), parts along dimension 1, may hold values from 0 to 1, as said below
- point_depth: float32 [4, 8, 384], P(None, ('group', 'dp')), parts along dimension 1, may hold values from -6 to 6
- hook_section: int32 [4], replicated, may hold values from 0 to 2, as said below
- w_query: bfloat16 [4, 1600, 832], P('section')
- w_key: bfloat16 [4, 1600, 832], P('section')
- w_value: bfloat16 [4, 1600, 832], P('section'), may hold values from -0.15625 to 0.15625
- w_output: bfloat16 [4, 832, 1600], P('section'), may hold values from -0.21875 to 0.21875
- reassemble: bfloat16 [5, 1600, 128], P(None, None, ('section', 'dp')), may hold values from -0.15625 to 0.15625
- merging: bfloat16 [4, 128, 128], P(None, None, ('section', 'dp')), may hold values from -0.5 to 0.5
- predict: bfloat16 [128, 196], P(('section', 'dp')), may hold values from -0.5 to 0.5
Outputs:
- grad_query: bfloat16 [8, 1600, 832], P(('group', 'section'), 'dp'), parts along dimension 0
- grad_key: bfloat16 [8, 1600, 832], P(('group', 'section'), 'dp'), parts along dimension 0
- grad_value: bfloat16 [8, 1600, 832], P(('group', 'section'), 'dp'), parts along dimension 0
- grad_output: bfloat16 [8, 832, 1600], P(('group', 'section'), 'dp'), parts along dimension 0
- grad_reassemble: float32 [10, 1600, 128], P('group', None, ('section', 'dp')), parts along dimension 0
- grad_merging: float32 [8, 128, 128], P('group', None, ('section', 'dp')), parts along dimension 0
- grad_predict: float32 [256, 196], P(('group', 'section', 'dp')), parts along dimension 0
There are 2 independent parts, one for each index of `group`. A program takes and returns all parts, laid end to end along the dimension named above; an argument that names none is the same for every part. Nothing has to cross between parts.
Inputs may be any that keep to these rules, and one draw needn't show every extreme that they name: `point_mask`: in each image the valid points come first, and at least 48 of them are valid. `hook_section`: Sorted; the last entry is 2.
All inputs are finite; a program needn't handle non-finite values.
Results may differ from a plain program's by a relative error of at most 0.03.
Values may be sent and summed in bfloat16 or wider, within the bound.
A program may use at most 128 MiB of HBM per device.

v0:
```python
import math
import jax
import jax.numpy as jnp
from jax import lax
from jax.sharding import PartitionSpec as P

HEADS = 13
NHOOK = 4
EPS = 1e-06


def passed_along(block, axis, distance):
    devices = range(lax.axis_size(axis))
    route = [(i - distance, i) for i in devices if i - distance in devices]
    return lax.ppermute(block, axis, route)


def broadcast(value, axis, source):
    kept = jnp.where(lax.axis_index(axis) == source, value, 0).astype(value.dtype)
    return lax.psum(kept, axis)


def as_sent(x):
    return jax.tree.map(lambda a: a.astype(jnp.bfloat16) if a.dtype == jnp.float32 else a, x)


def rms_normed(stream):
    widened = stream.astype(jnp.float32)
    inv_root = lax.rsqrt(jnp.mean(widened * widened, axis=-1, keepdims=True) + EPS)
    return (widened * inv_root).astype(jnp.bfloat16)


def attend(query_rows, key_rows, value_rows):
    image_count, token_count, inner_width = query_rows.shape
    head_width = inner_width // HEADS
    shape_heads = (image_count, token_count, HEADS, head_width)
    query_heads = query_rows.astype(jnp.float32).reshape(shape_heads)
    key_heads = key_rows.astype(jnp.float32).reshape(shape_heads)
    value_heads = value_rows.astype(jnp.float32).reshape(shape_heads)
    scores = jnp.einsum("bqhe,bkhe->bhqk", query_heads, key_heads) / math.sqrt(head_width)
    probabilities = jax.nn.softmax(scores, axis=-1).astype(jnp.bfloat16)
    mixed_heads = jnp.einsum("bhqk,bkhe->bqhe", probabilities.astype(jnp.float32), value_heads)
    return mixed_heads.reshape(image_count, token_count, inner_width).astype(jnp.bfloat16)


def attention_layer(stream, layer_query, layer_key, layer_value, layer_output, nudges):
    image_count, token_count, model_width = stream.shape
    normed = rms_normed(stream).reshape(image_count * token_count, model_width)
    query_rows = (
        jnp.dot(normed, layer_query, preferred_element_type=jnp.float32).astype(jnp.bfloat16)
        + nudges[0]
    )
    key_rows = (
        jnp.dot(normed, layer_key, preferred_element_type=jnp.float32).astype(jnp.bfloat16)
        + nudges[1]
    )
    value_rows = (
        jnp.dot(normed, layer_value, preferred_element_type=jnp.float32).astype(jnp.bfloat16)
        + nudges[2]
    )
    inner_width = layer_query.shape[1]
    mixed = attend(
        query_rows.reshape(image_count, token_count, inner_width),
        key_rows.reshape(image_count, token_count, inner_width),
        value_rows.reshape(image_count, token_count, inner_width),
    )
    mixed_rows = mixed.reshape(image_count * token_count, inner_width)
    update = jnp.dot(mixed_rows, layer_output, preferred_element_type=jnp.float32)
    update = update.reshape(image_count, token_count, model_width)
    output_rows = stream.astype(jnp.float32) + update
    return (output_rows, (normed, mixed_rows))


def reassemble_map(features, weight):
    flat_rows = features.reshape(-1, features.shape[-1]).astype(jnp.bfloat16)
    return jnp.dot(flat_rows, weight, preferred_element_type=jnp.float32).astype(jnp.bfloat16)


def head_rest(projected, top_projected, merging, predict, pixel_index, point_mask, point_depth):
    merged = top_projected.astype(jnp.float32)
    for hook_slot in range(len(projected) - 1, -1, -1):
        activated = jax.nn.silu(merged).astype(jnp.bfloat16)
        merged = projected[hook_slot].astype(jnp.float32) + jnp.dot(
            activated, merging[hook_slot], preferred_element_type=jnp.float32
        )
    activated = jax.nn.silu(merged).astype(jnp.bfloat16)
    depth_rows = jnp.dot(activated, predict, preferred_element_type=jnp.float32)
    depth_map = depth_rows.reshape(pixel_index.shape[0], pixel_index.shape[1], -1)
    picked = jnp.take_along_axis(depth_map, pixel_index, axis=2)
    valid_mask = point_mask.astype(jnp.float32)
    valid_count = jnp.sum(valid_mask, axis=2)
    misfit = (picked - point_depth) * valid_mask
    return jnp.sum(jnp.sum(misfit * misfit, axis=2) / valid_count)


def keep_rows(stream):
    return stream


def put_slot(store_array, item_rows, micro_slot, active):
    updated = lax.dynamic_update_index_in_dim(store_array, item_rows, micro_slot, 0)
    return jnp.where(active, updated, store_array)


def contract(left_rows, right_rows):
    return jnp.einsum("mrd,mrh->dh", left_rows, right_rows, preferred_element_type=jnp.float32)


def on_device(
    tokens,
    pixel_index,
    point_mask,
    point_depth,
    hook_section,
    w_query,
    w_key,
    w_value,
    w_output,
    reassemble,
    merging,
    predict,
):
    section_index = lax.axis_index("section")
    section_count = lax.axis_size("section")
    last_section = section_count - 1
    is_last = section_index == last_section
    micro_count = tokens.shape[0]
    token_rows = tokens.shape[1] * tokens.shape[2]
    model_width = tokens.shape[3]
    inner_width = w_query.shape[2]
    layer_query = w_query[0]
    layer_key = w_key[0]
    layer_value = w_value[0]
    layer_output = w_output[0]
    full_reassemble, full_merging, full_predict = (
        lax.all_gather(reassemble, ("section", "dp"), axis=2, tiled=True),
        lax.all_gather(merging, ("section", "dp"), axis=2, tiled=True),
        lax.all_gather(predict, ("section", "dp"), axis=0, tiled=True),
    )
    zero_nudges = jnp.zeros((3, token_rows, inner_width), jnp.bfloat16)
    zero_rows = jnp.zeros(tokens.shape[1:], jnp.float32)
    empty_store = jnp.zeros(tokens.shape, jnp.float32)

    def run_layer(stream):
        return attention_layer(
            stream, layer_query, layer_key, layer_value, layer_output, zero_nudges
        )[0]

    def forward_step(time_step, carried):
        incoming, inputs_store, outputs_store = carried
        micro_index = time_step - section_index
        active = jnp.logical_and(micro_index >= 0, micro_index < micro_count)
        micro_slot = jnp.clip(micro_index, 0, micro_count - 1)
        fresh_rows = lax.dynamic_index_in_dim(tokens, micro_slot, 0, keepdims=False).astype(
            jnp.float32
        )
        source = jnp.where(section_index == 0, fresh_rows, incoming)
        result = lax.cond(active, run_layer, keep_rows, source)
        inputs_store = put_slot(inputs_store, source, micro_slot, active)
        outputs_store = put_slot(outputs_store, result, micro_slot, active)
        incoming = passed_along(result, "section", 1)
        return (incoming, inputs_store, outputs_store)

    unused, inputs_store, outputs_store = lax.fori_loop(
        0, micro_count + section_count - 1, forward_step, (zero_rows, empty_store, empty_store)
    )
    hook_sum = jnp.zeros(tokens.shape, jnp.float32)
    received = []
    for hook_slot in range(NHOOK):
        local_piece = reassemble_map(outputs_store, full_reassemble[hook_slot])
        received.append(broadcast(local_piece, "section", hook_section[hook_slot]))
    projected_in = tuple(received)

    def head_grads(head_items):

        def loss_terms(projected, top_feature, reassemble_last, head_merging, head_predict):
            top_projected = reassemble_map(top_feature, reassemble_last)
            return head_rest(
                projected,
                top_projected,
                head_merging,
                head_predict,
                pixel_index,
                point_mask,
                point_depth,
            )

        loss_value, pullback = jax.vjp(
            loss_terms,
            head_items[0],
            head_items[1],
            full_reassemble[NHOOK],
            full_merging,
            full_predict,
        )
        return pullback(jnp.ones((), jnp.float32))

    def no_grads(head_items):
        return (
            tuple((jnp.zeros_like(array_item) for array_item in head_items[0])),
            jnp.zeros_like(head_items[1]),
            jnp.zeros_like(full_reassemble[NHOOK]),
            jnp.zeros_like(full_merging),
            jnp.zeros_like(full_predict),
        )

    projected_grads, last_grad, reassemble_last_grad, grad_merging, grad_predict = lax.cond(
        is_last, head_grads, no_grads, (projected_in, outputs_store)
    )
    projected_cotangents = broadcast(jnp.stack(projected_grads), "section", last_section)
    weight_grads = []
    for hook_slot in range(NHOOK):
        unused_rows, pullback = jax.vjp(reassemble_map, outputs_store, full_reassemble[hook_slot])
        feature_grad, weight_grad = pullback(projected_cotangents[hook_slot])
        is_owner = hook_section[hook_slot] == section_index
        hook_sum = hook_sum + jnp.where(is_owner, feature_grad, 0.0)
        weight_grads.append(jnp.where(is_owner, weight_grad, jnp.zeros_like(weight_grad)))
    weight_grads.append(reassemble_last_grad)
    grad_reassemble = jnp.stack(weight_grads)
    hook_grad = hook_sum

    def backward_one(stream, cotangent):

        def local_layer(entry_rows, nudges):
            return attention_layer(
                entry_rows, layer_query, layer_key, layer_value, layer_output, nudges
            )

        unused_rows, pullback, saved = jax.vjp(local_layer, stream, zero_nudges, has_aux=True)
        entry_grad, nudge_grad = pullback(cotangent)
        return (entry_grad, nudge_grad, saved[0], saved[1])

    def skip_one(stream, cotangent):
        return (
            jnp.zeros_like(stream),
            zero_nudges,
            jnp.zeros((token_rows, model_width), jnp.bfloat16),
            jnp.zeros((token_rows, inner_width), jnp.bfloat16),
        )

    def backward_step(time_step, carried):
        incoming, nudge_store, normed_store, mixed_store, cotangent_store = carried
        micro_index = time_step - (last_section - section_index)
        active = jnp.logical_and(micro_index >= 0, micro_index < micro_count)
        micro_slot = jnp.clip(micro_index, 0, micro_count - 1)
        upstream = jnp.where(
            is_last, lax.dynamic_index_in_dim(last_grad, micro_slot, 0, keepdims=False), incoming
        )
        cotangent = upstream + lax.dynamic_index_in_dim(hook_grad, micro_slot, 0, keepdims=False)
        stream = lax.dynamic_index_in_dim(inputs_store, micro_slot, 0, keepdims=False)
        entry_grad, nudge_grad, normed, mixed_rows = lax.cond(
            active, backward_one, skip_one, stream, cotangent
        )
        nudge_store = put_slot(nudge_store, nudge_grad, micro_slot, active)
        normed_store = put_slot(normed_store, normed, micro_slot, active)
        mixed_store = put_slot(mixed_store, mixed_rows, micro_slot, active)
        cotangent_store = put_slot(cotangent_store, cotangent, micro_slot, active)
        incoming = jax.tree.map(
            lambda part, own: part.astype(own.dtype),
            passed_along(as_sent(entry_grad), "section", -1),
            entry_grad,
        )
        return (incoming, nudge_store, normed_store, mixed_store, cotangent_store)

    start_state = (
        zero_rows,
        jnp.zeros((micro_count, 3, token_rows, inner_width), jnp.bfloat16),
        jnp.zeros((micro_count, token_rows, model_width), jnp.bfloat16),
        jnp.zeros((micro_count, token_rows, inner_width), jnp.bfloat16),
        empty_store,
    )
    unused, nudge_store, normed_store, mixed_store, cotangent_store = lax.fori_loop(
        0, micro_count + section_count - 1, backward_step, start_state
    )
    grad_query = contract(normed_store, nudge_store[:, 0])
    grad_key = contract(normed_store, nudge_store[:, 1])
    grad_value = contract(normed_store, nudge_store[:, 2])
    mixed_all = mixed_store.reshape(micro_count * token_rows, inner_width)
    update_grad = cotangent_store.reshape(micro_count * token_rows, model_width)

    def output_map(weight):
        return jnp.dot(mixed_all, weight, preferred_element_type=jnp.float32)

    unused_update, output_pullback = jax.vjp(output_map, layer_output)
    grad_output = output_pullback(update_grad)[0].astype(jnp.float32)
    summed_query, summed_key, summed_value, summed_output = (
        lax.psum_scatter(
            grad_query[None].astype(jnp.bfloat16), "dp", scatter_dimension=1, tiled=True
        ).astype(jnp.float32),
        lax.psum_scatter(
            grad_key[None].astype(jnp.bfloat16), "dp", scatter_dimension=1, tiled=True
        ).astype(jnp.float32),
        lax.psum_scatter(
            grad_value[None].astype(jnp.bfloat16), "dp", scatter_dimension=1, tiled=True
        ).astype(jnp.float32),
        lax.psum_scatter(
            grad_output[None].astype(jnp.bfloat16), "dp", scatter_dimension=1, tiled=True
        ).astype(jnp.float32),
    )
    head_reassemble, head_merging, head_predict = (
        lax.psum_scatter(
            grad_reassemble.astype(jnp.float32), ("section", "dp"), scatter_dimension=2, tiled=True
        ),
        lax.psum_scatter(
            grad_merging.astype(jnp.float32), ("section", "dp"), scatter_dimension=2, tiled=True
        ),
        lax.psum_scatter(
            grad_predict.astype(jnp.float32), ("section", "dp"), scatter_dimension=0, tiled=True
        ),
    )
    return (
        summed_query.astype(jnp.bfloat16),
        summed_key.astype(jnp.bfloat16),
        summed_value.astype(jnp.bfloat16),
        summed_output.astype(jnp.bfloat16),
        head_reassemble,
        head_merging,
        head_predict,
    )


def solution(mesh):
    placed = (
        P(None, ("group", "dp"), None, None),
        P(None, ("group", "dp"), None),
        P(None, ("group", "dp"), None),
        P(None, ("group", "dp"), None),
        P(),
        P("section", None, None),
        P("section", None, None),
        P("section", None, None),
        P("section", None, None),
        P(None, None, ("section", "dp")),
        P(None, None, ("section", "dp")),
        P(("section", "dp"), None),
    )
    return jax.shard_map(
        on_device,
        mesh=mesh,
        in_specs=placed,
        out_specs=(
            P(("group", "section"), "dp", None),
            P(("group", "section"), "dp", None),
            P(("group", "section"), "dp", None),
            P(("group", "section"), "dp", None),
            P("group", None, ("section", "dp")),
            P("group", None, ("section", "dp")),
            P(("group", "section", "dp"), None),
        ),
        check_vma=False,
    )
```

profile of v0, /device:TPU:0, one launch (start us, length us, event | category | flops | bytes accessed | tf_op | source)
XLA Modules:
  0.0 981.0 jit_solution(7728629565180497052)
XLA Ops:
  14.5 4.3 copy.215
  18.8 5.3 copy.216
  24.1 5.3 copy.214
  30.4 131.4 %while.42 = (s32[]{:T(128)}, f32[1,32,1600]{2,1,0:T(8,128)S(1)}, f32[4,1,32,1600]{3,2,1,0:T(8,128)}, bf16[4,1,32,1600]{3,2,1,0:T(8,128)(2,1)}, s32[]{:T(128)}, /...) while((s32[]{:T(128)}, f32[1,32,1600]{2,1,0:T(8,128)S(1)}, ...), condition=%wide.region_6.7_spmd, body=%wide.region_0.6_spmd.sunk | while | flops 344828992 | bytes 25776712 | solution.py:164
  32.1 10.4 %conditional.7 = (f32[1,32,1600]{2,1,0:T(8,128)S(1)}) conditional(s32[]{:T(128)} %convert_element_type.778, f32[1,32,1600]{2,1,0:T(8,128)S(1)} %get-tuple-element.1149, (f32[1,32,1600]{2,1,0:T(8,128)S(1)}, bf16[1600,832]{1,0:T(8,128)(2,1)}, bf16[1600,832]{1,0:T(8,128)(2,1)S(1)}, bf16[1600,832]{1,0:T(8,128)(2,1)}, bf16[832,1600]{1,0:T(8,128)(2,1)}) %tuple.167), branch_computations={%region_1.1_spmd, %region_2.5_spmd} | conditional | flops 344624192 | bytes 23596836 | solution.py:158
  45.4 7.6 collective-permute-done
  54.7 10.4 %conditional.7 = (f32[1,32,1600]{2,1,0:T(8,128)S(1)}) conditional(s32[]{:T(128)} %convert_element_type.778, f32[1,32,1600]{2,1,0:T(8,128)S(1)} %get-tuple-element.1149, (f32[1,32,1600]{2,1,0:T(8,128)S(1)}, bf16[1600,832]{1,0:T(8,128)(2,1)}, bf16[1600,832]{1,0:T(8,128)(2,1)S(1)}, bf16[1600,832]{1,0:T(8,128)(2,1)}, bf16[832,1600]{1,0:T(8,128)(2,1)}) %tuple.167), branch_computations={%region_1.1_spmd, %region_2.5_spmd} | conditional | flops 344624192 | bytes 23596836 | solution.py:158
  65.1 4.4 collective-permute-start
  71.1 3.2 collective-permute-done
  76.0 10.4 %conditional.7 = (f32[1,32,1600]{2,1,0:T(8,128)S(1)}) conditional(s32[]{:T(128)} %convert_element_type.778, f32[1,32,1600]{2,1,0:T(8,128)S(1)} %get-tuple-element.1149, (f32[1,32,1600]{2,1,0:T(8,128)S(1)}, bf16[1600,832]{1,0:T(8,128)(2,1)}, bf16[1600,832]{1,0:T(8,128)(2,1)S(1)}, bf16[1600,832]{1,0:T(8,128)(2,1)}, bf16[832,1600]{1,0:T(8,128)(2,1)}) %tuple.167), branch_computations={%region_1.1_spmd, %region_2.5_spmd} | conditional | flops 344624192 | bytes 23596836 | solution.py:158
  86.4 4.4 collective-permute-start
  96.4 10.4 %conditional.7 = (f32[1,32,1600]{2,1,0:T(8,128)S(1)}) conditional(s32[]{:T(128)} %convert_element_type.778, f32[1,32,1600]{2,1,0:T(8,128)S(1)} %get-tuple-element.1149, (f32[1,32,1600]{2,1,0:T(8,128)S(1)}, bf16[1600,832]{1,0:T(8,128)(2,1)}, bf16[1600,832]{1,0:T(8,128)(2,1)S(1)}, bf16[1600,832]{1,0:T(8,128)(2,1)}, bf16[832,1600]{1,0:T(8,128)(2,1)}) %tuple.167), branch_computations={%region_1.1_spmd, %region_2.5_spmd} | conditional | flops 344624192 | bytes 23596836 | solution.py:158
  106.8 4.4 collective-permute-start
  116.2 14.8 %collective-permute-start = (f32[1,32,1600]{2,1,0:T(8,128)S(1)}, f32[1,32,1600]{2,1,0:T(8,128)S(1)}, u32[]{:S(2)}, u32[]{:S(2)}) collective-permute-start(f32[1,32,1600]{2,1,0:T(8,128)S(1)} %get-tuple-element.1302), channel_id=1, source_target_pairs={{0,4},{4,8},{8,12},{1,5},{5,9},{9,13},{2,6},{6,10},{10,14},{3,7},{... | collective-permute-start | bytes 614408 | tf_op jit(solution)/shard_map/while/body/eval_jaxpr/ppermute | solution.py:15
  136.1 4.4 collective-permute-start
  145.5 12.9 %collective-permute-start = (f32[1,32,1600]{2,1,0:T(8,128)S(1)}, f32[1,32,1600]{2,1,0:T(8,128)S(1)}, u32[]{:S(2)}, u32[]{:S(2)}) collective-permute-start(f32[1,32,1600]{2,1,0:T(8,128)S(1)} %get-tuple-element.1302), channel_id=1, source_target_pairs={{0,4},{4,8},{8,12},{1,5},{5,9},{9,13},{2,6},{6,10},{10,14},{3,7},{... | collective-permute-start | bytes 614408 | tf_op jit(solution)/shard_map/while/body/eval_jaxpr/ppermute | solution.py:15
  170.1 31.5 %all_gather.11 = bf16[128,196]{1,0:T(8,128)(2,1)S(1)} all-gather(bf16[8,196]{1,0:T(8,128)(2,1)S(1)} %copy-done.20), channel_id=1, replica_groups=mesh['group'=2,'section'=4,'dp'=4] {'section','dp'}, dimensions={0}, use_global_device_ids=true | all-gather | bytes 53312 | tf_op jit(solution)/shard_map/all_gather | solution.py:138
  201.6 17.9 %all_gather.10 = bf16[4,128,128]{1,0,2:T(4,128)(2,1)S(1)} all-gather(bf16[4,128,8]{1,0,2:T(4,128)(2,1)S(1)} %copy.217), channel_id=1, replica_groups=mesh['group'=2,'section'=4,'dp'=4] {'section','dp'}, dimensions={2}, use_global_device_ids=true | all-gather | bytes 139264 | tf_op jit(solution)/shard_map/all_gather | solution.py:137
  219.5 4.9 conditional.3
  228.7 75.9 %all-reduce.11.cloned.1.call-done = bf16[4,128,128]{2,1,0:T(8,128)(2,1)} async-done(((bf16[4,128,128]{2,1,0:T(8,128)(2,1)}), bf16[4,128,128]{2,1,0:T(8,128)(2,1)}) %all-reduce.11.cloned.1.call-update) | async-done | bytes 131088 | tf_op jit(solution)/shard_map/psum | solution.py:20
  315.7 278.6 %while.43 = (s32[]{:T(128)}, f32[1,32,1600]{2,1,0:T(8,128)S(1)}, bf16[4,3,32,832]{3,2,0,1:T(8,128)(2,1)}, bf16[4,32,1600]{2,1,0:T(8,128)(2,1)}, bf16[4,32,832]{2...) while((s32[]{:T(128)}, f32[1,32,1600]{2,1,0:T(8,128)S(1)}, ...), condition=%wide.region_24.25_spmd.clone, body=%wide.region_16.24_spmd.clone.sunk | while | flops 608857152 | bytes 61259056 | solution.py:272
  344.9 87.1 %collective-permute-done.1 = bf16[1,32,1600]{2,1,0:T(8,128)(2,1)S(1)} collective-permute-done((bf16[1,32,1600]{2,1,0:T(8,128)(2,1)}, bf16[1,32,1600]{2,1,0:T(8,128)(2,1)S(1)}, u32[]{:S(2)}, u32[]{:S(2)}) %collective-permute-start.1) | collective-permute-done | bytes 102432 | tf_op jit(solution)/shard_map/while/body/eval_jaxpr/ppermute | solution.py:15
  433.8 31.3 %conditional.8 = (bf16[1,32,1600]{2,1,0:T(8,128)(2,1)}, bf16[1,3,32,832]{3,2,1,0:T(8,128)(2,1)S(1)}, bf16[1,32,1600]{2,1,0:T(8,128)(2,1)}, bf16[1,32,832]{2,1,0:T(8,128)(2,1)S(1)}) conditional(s32[]{:T(128)} %convert_element_type.779, () %tuple.170, (f32[1,32,1600]{2,1,0:T(8,128)S(1)}, bf16[832,1600]{1,0:T(8,128)(2,1)}, ...), branch_computations={%region_17.17_spmd, %region_18.23_spmd} | conditional | flops 608443456 | bytes 57541052 | solution.py:251
  435.0 2.5 convolution_convert_fusion.13
  458.3 2.9 convolution_convert_fusion.5
  474.6 31.3 %conditional.8 = (bf16[1,32,1600]{2,1,0:T(8,128)(2,1)}, bf16[1,3,32,832]{3,2,1,0:T(8,128)(2,1)S(1)}, bf16[1,32,1600]{2,1,0:T(8,128)(2,1)}, bf16[1,32,832]{2,1,0:T(8,128)(2,1)S(1)}) conditional(s32[]{:T(128)} %convert_element_type.779, () %tuple.170, (f32[1,32,1600]{2,1,0:T(8,128)S(1)}, bf16[832,1600]{1,0:T(8,128)(2,1)}, ...), branch_computations={%region_17.17_spmd, %region_18.23_spmd} | conditional | flops 608443456 | bytes 57541052 | solution.py:251
  475.8 2.5 convolution_convert_fusion.13
  499.1 2.9 convolution_convert_fusion.5
  515.3 31.3 %conditional.8 = (bf16[1,32,1600]{2,1,0:T(8,128)(2,1)}, bf16[1,3,32,832]{3,2,1,0:T(8,128)(2,1)S(1)}, bf16[1,32,1600]{2,1,0:T(8,128)(2,1)}, bf16[1,32,832]{2,1,0:T(8,128)(2,1)S(1)}) conditional(s32[]{:T(128)} %convert_element_type.779, () %tuple.170, (f32[1,32,1600]{2,1,0:T(8,128)S(1)}, bf16[832,1600]{1,0:T(8,128)(2,1)}, ...), branch_computations={%region_17.17_spmd, %region_18.23_spmd} | conditional | flops 608443456 | bytes 57541052 | solution.py:251
  516.5 2.5 convolution_convert_fusion.13
  539.8 2.9 convolution_convert_fusion.5
  556.0 31.3 %conditional.8 = (bf16[1,32,1600]{2,1,0:T(8,128)(2,1)}, bf16[1,3,32,832]{3,2,1,0:T(8,128)(2,1)S(1)}, bf16[1,32,1600]{2,1,0:T(8,128)(2,1)}, bf16[1,32,832]{2,1,0:T(8,128)(2,1)S(1)}) conditional(s32[]{:T(128)} %convert_element_type.779, () %tuple.170, (f32[1,32,1600]{2,1,0:T(8,128)S(1)}, bf16[832,1600]{1,0:T(8,128)(2,1)}, ...), branch_computations={%region_17.17_spmd, %region_18.23_spmd} | conditional | flops 608443456 | bytes 57541052 | solution.py:251
  557.2 2.5 convolution_convert_fusion.13
  580.5 2.9 convolution_convert_fusion.5
  596.3 12.4 %copy.242 = bf16[1,1600,832]{2,0,1:T(2,128)(2,1)} copy(bf16[1,1600,832]{1,2,0:T(8,128)(2,1)S(1)} %fusion.92) | data formatting | bytes 5324800
  608.8 4.7 copy.332
  617.2 14.5 %copy.244 = bf16[1,1600,832]{2,0,1:T(2,128)(2,1)} copy(bf16[1,1600,832]{1,2,0:T(8,128)(2,1)} %fusion.93) | data formatting | bytes 5324800
  631.7 4.6 copy.331
  639.1 14.4 %copy.240 = bf16[1,1600,832]{2,0,1:T(2,128)(2,1)} copy(bf16[1,1600,832]{1,2,0:T(8,128)(2,1)} %fusion.91) | data formatting | bytes 5324800
  653.5 4.6 copy.333
  664.7 4.8 copy.229
  673.1 3.4 fusion.90
  679.4 8.6 reduce-scatter.26.cloned.1.call-done
  690.7 35.9 %reduce-scatter.22.cloned.1.call-done = bf16[400,832]{1,0:T(8,128)(2,1)} async-done(((bf16[1600,832]{1,0:T(8,128)(2,1)}), bf16[400,832]{1,0:T(8,128)(2,1)}) %reduce-scatter.22.cloned.1.call-update) | async-done | bytes 665616
  729.4 90.1 %reduce-scatter.18.cloned.1.call-done = f32[5,1600,8]{1,0,2:T(8,128)} async-done(((f32[5,1600,128]{1,0,2:T(8,128)}), f32[5,1600,8]{1,0,2:T(8,128)}) %reduce-scatter.18.cloned.1.call-update) | async-done | bytes 256016 | tf_op jit(solution)/shard_map/reduce_scatter | solution.py:301
  821.3 56.8 %reduce-scatter.28.cloned.1.call-done = f32[8,196]{1,0:T(8,128)} async-done(((f32[128,196]{1,0:T(8,128)}), f32[8,196]{1,0:T(8,128)}) %reduce-scatter.28.cloned.1.call-update) | async-done | bytes 6288
  878.1 58.5 %reduce-scatter.20.cloned.1.call-done = f32[4,128,8]{1,2,0:T(8,128)} async-done(((f32[4,128,128]{1,2,0:T(8,128)}), f32[4,128,8]{1,2,0:T(8,128)}) %reduce-scatter.20.cloned.1.call-update) | async-done | bytes 16400 | tf_op jit(solution)/shard_map/reduce_scatter | solution.py:304
  936.6 37.6 %reduce-scatter.16.cloned.1.call-done = bf16[1,208,1600]{2,1,0:T(8,128)(2,1)} async-done(((bf16[1,832,1600]{2,1,0:T(8,128)(2,1)}), bf16[1,208,1600]{2,1,0:T(8,128)(2,1)}) %reduce-scatter.16.cloned.1.call-update) | async-done | bytes 665616 | tf_op jit(solution)/shard_map/reduce_scatter | solution.py:296
  (440 shorter events, 308.1 us)
Async XLA Ops:
  7.2 154.6 %all-gather.2.cloned.1.call-start = ((), (), s32[]{:S(2)}) async-start(), calls=%async_computation.7 | async-start | bytes 2263040 | tf_op jit(solution)/shard_map/all_gather | solution.py:136
  7.9 211.6 %all-reduce.13.cloned.1.call-start = ((), (), s32[]{:S(2)}) async-start(), calls=%async_computation.16 | async-start | bytes 262144 | tf_op jit(solution)/shard_map/psum | solution.py:20
  42.5 10.5 %collective-permute-start = (f32[1,32,1600]{2,1,0:T(8,128)S(1)}, f32[1,32,1600]{2,1,0:T(8,128)S(1)}, u32[]{:S(2)}, u32[]{:S(2)}) collective-permute-start(f32[1,32,1600]{2,1,0:T(8,128)S(1)} %get-tuple-element.1302), channel_id=1, source_target_pairs={{0,4},{4,8},{8,12},{1,5},{5,9},{9,13},{2,6},{6,10},{10,14},{3,7},{... | collective-permute-start | bytes 614408 | tf_op jit(solution)/shard_map/while/body/eval_jaxpr/ppermute | solution.py:15
  65.1 9.2 collective-permute-start
  86.4 8.3 collective-permute-start
  106.8 7.7 collective-permute-start
  116.2 18.1 %collective-permute-start = (f32[1,32,1600]{2,1,0:T(8,128)S(1)}, f32[1,32,1600]{2,1,0:T(8,128)S(1)}, u32[]{:S(2)}, u32[]{:S(2)}) collective-permute-start(f32[1,32,1600]{2,1,0:T(8,128)S(1)} %get-tuple-element.1302), channel_id=1, source_target_pairs={{0,4},{4,8},{8,12},{1,5},{5,9},{9,13},{2,6},{6,10},{10,14},{3,7},{... | collective-permute-start | bytes 614408 | tf_op jit(solution)/shard_map/while/body/eval_jaxpr/ppermute | solution.py:15
  136.1 7.7 collective-permute-start
  145.5 16.2 %collective-permute-start = (f32[1,32,1600]{2,1,0:T(8,128)S(1)}, f32[1,32,1600]{2,1,0:T(8,128)S(1)}, u32[]{:S(2)}, u32[]{:S(2)}) collective-permute-start(f32[1,32,1600]{2,1,0:T(8,128)S(1)} %get-tuple-element.1302), channel_id=1, source_target_pairs={{0,4},{4,8},{8,12},{1,5},{5,9},{9,13},{2,6},{6,10},{10,14},{3,7},{... | collective-permute-start | bytes 614408 | tf_op jit(solution)/shard_map/while/body/eval_jaxpr/ppermute | solution.py:15
  161.7 8.3 copy-start.18
  161.7 8.3 copy-start.20
  161.7 57.7 %copy-start.16 = (s32[4,1,384]{2,1,0:T(1,128)S(1)}, s32[4,1,384]{2,1,0:T(1,128)}, u32[]{:S(2)}) copy-start(s32[4,1,384]{2,1,0:T(1,128)} %param.23) | copy-start | bytes 18436
  161.7 57.7 %copy-start.17 = (s32[4,1,384]{2,1,0:T(1,128)S(1)}, s32[4,1,384]{2,1,0:T(1,128)}, u32[]{:S(2)}) copy-start(s32[4,1,384]{2,1,0:T(1,128)} %param.24) | copy-start | bytes 18436
  161.8 57.7 %copy-start.19 = (f32[4,1,384]{2,1,0:T(1,128)S(1)}, f32[4,1,384]{2,1,0:T(1,128)}, u32[]{:S(2)}) copy-start(f32[4,1,384]{2,1,0:T(1,128)} %param.25) | copy-start | bytes 18436
  170.0 134.6 %all-reduce.11.cloned.1.call-start = ((), (), s32[]{:S(2)}) async-start(), calls=%async_computation.8 | async-start | bytes 262144 | tf_op jit(solution)/shard_map/psum | solution.py:20
  224.3 3.7 copy-start.10
  226.0 450.6 %reduce-scatter.24.cloned.1.call-start = ((), (), s32[]{:S(2)}) async-start(), calls=%async_computation.13 | async-start | bytes 3584000
  318.8 6.8 collective-permute-start.1
  328.8 6.8 collective-permute-start.1
  338.9 93.1 %collective-permute-start.1 = (bf16[1,32,1600]{2,1,0:T(8,128)(2,1)}, bf16[1,32,1600]{2,1,0:T(8,128)(2,1)S(1)}, u32[]{:S(2)}, u32[]{:S(2)}) collective-permute-start(bf16[1,32,1600]{2,1,0:T(8,128)(2,1)} %get-tuple-element.1167), channel_id=1, source_target_pairs={{4,0},{8,4},{12,8},{5,1},{9,5},{13,9},{6,2},{10,6},{14,10},{7,3},{... | collective-permute-start | bytes 307208 | tf_op jit(solution)/shard_map/while/body/eval_jaxpr/ppermute | solution.py:15
  433.8 3.7 copy-start.1
  437.6 3.2 copy-start.3
  461.2 3.8 copy-start.7
  461.3 3.8 copy-start.8
  465.1 7.6 collective-permute-start.1
  474.6 3.7 copy-start.1
  478.3 3.2 copy-start.3
  502.0 3.8 copy-start.7
  502.0 3.8 copy-start.8
  505.9 7.6 collective-permute-start.1
  515.3 3.7 copy-start.1
  519.0 3.2 copy-start.3
  542.7 3.8 copy-start.7
  542.7 3.8 copy-start.8
  546.6 7.6 collective-permute-start.1
  556.0 3.7 copy-start.1
  559.8 3.2 copy-start.3
  583.5 3.8 copy-start.7
  583.5 3.8 copy-start.8
  587.3 7.0 collective-permute-start.1
  613.5 74.4 %reduce-scatter.26.cloned.1.call-start = ((), (), s32[]{:S(2)}) async-start(), calls=%async_computation.14 | async-start | bytes 3584000
  636.4 90.3 %reduce-scatter.22.cloned.1.call-start = ((), (), s32[]{:S(2)}) async-start(), calls=%async_computation.12 | async-start | bytes 3584000
  658.1 6.5 copy-start.11
  658.2 161.4 %reduce-scatter.18.cloned.1.call-start = ((), (), s32[]{:S(2)}) async-start(), calls=%async_computation.10 | async-start | bytes 7241728 | tf_op jit(solution)/shard_map/reduce_scatter | solution.py:301
  669.5 3.6 copy-start.9
  669.5 208.6 %reduce-scatter.28.cloned.1.call-start = ((), (), s32[]{:S(2)}) async-start(), calls=%async_computation.15 | async-start | bytes 139264
  671.2 265.4 %reduce-scatter.20.cloned.1.call-start = ((), (), s32[]{:S(2)}) async-start(), calls=%async_computation.11 | async-start | bytes 278528 | tf_op jit(solution)/shard_map/reduce_scatter | solution.py:304
  673.0 301.2 %reduce-scatter.16.cloned.1.call-start = ((), (), s32[]{:S(2)}) async-start(), calls=%async_computation.9 | async-start | bytes 3461120 | tf_op jit(solution)/shard_map/reduce_scatter | solution.py:296
  (19 other events, 38.9 us)
Sparse Core Ops, SparseCore 0:
  10.2 44.1 all-gather.1
  170.1 45.8 all-reduce.12
  226.1 78.4 all-reduce.10
  613.6 35.4 reduce-scatter.23
  651.7 36.2 reduce-scatter.25
  690.3 36.2 reduce-scatter.21
  731.1 88.3 reduce-scatter.17
  823.6 54.5 reduce-scatter.27
  882.2 54.3 reduce-scatter.19
  939.6 34.5 reduce-scatter.15
where the time goes:
time: 987 us; the launch traced here: 981 us
  waiting for transfers between devices  475 us (48%)
  matrix products  149 us (15%)
  local copies, waits for them, and re-layouts  142 us (14%)
  other arithmetic  88.3 us (9%)
  starting transfers between devices  56.4 us (6%)
  blocking collectives  49.4 us (5%)
  between operations  19.4 us (2%)
    ppermute x14, waiting for transfers between devices, passed_along(): return lax.ppermute(block, axis, route)  111 us
    unnamed x14, waiting for transfers between devices  102 us
    reduce_scatter x1, waiting for transfers between devices, on_device(): lax.psum_scatter(grad_reassemble.astype(jnp.float32), ('section', 'dp'),...  90.1 us
    unnamed x43, local copies, waits for them, and re-layouts  85.7 us
    psum x2, waiting for transfers between devices, broadcast(): return lax.psum(kept, axis)  75.9 us
    select_n x42, other arithmetic, put_slot(): return jnp.where(active, updated, store_array)  65.6 us
    reduce_scatter x1, waiting for transfers between devices, on_device(): lax.psum_scatter(grad_merging.astype(jnp.float32), ('section', 'dp'), sca...  58.5 us
    ppermute x14, starting transfers between devices, passed_along(): return lax.ppermute(block, axis, route)  55.6 us
  transfers between devices with their start and end apart: 24, of which 20 were waited for; matrix products, arithmetic and copies ran while one was open for 20% of the time, Pallas kernels for 0%

commit v1 on v0

--- a/solution.py
+++ b/solution.py
@@ -7,6 +7,12 @@
 HEADS = 13
 NHOOK = 4
 EPS = 1e-06
+
+
+def _return_all_cycles(here_x, in_dim):
+    big = list(here_x.shape[1:])
+    big[in_dim] *= here_x.shape[0]
+    return jnp.moveaxis(here_x, 0, in_dim).reshape(big)
 
 
 def passed_along(block, axis, distance):
@@ -132,10 +138,34 @@
     layer_key = w_key[0]
     layer_value = w_value[0]
     layer_output = w_output[0]
+
+    def arrange_ratios(sheet, mesh_name, dimension_no):
+        n_axis = lax.axis_size(mesh_name)
+        block_list = [(c, (c + 1) % n_axis) for c in range(n_axis)]
+        ledger = [(u, kk) for kk, u in block_list]
+        j0 = 0
+        u1, t1 = ([], [])
+        while j0 < n_axis - 1:
+            if j0 % 2 == 0:
+                block_now = lax.ppermute(
+                    u1[-1] if u1 else sheet, axis_name=mesh_name, perm=block_list
+                )
+                u1.append(block_now)
+            else:
+                vec_out = lax.ppermute(t1[-1] if t1 else sheet, axis_name=mesh_name, perm=ledger)
+                t1.append(vec_out)
+            j0 += 1
+        val = jnp.stack([*u1[::-1], sheet, *t1], axis=0)
+        outcome_arr = len(u1)
+        o_now = lax.axis_index(mesh_name)
+        local_part = o_now - outcome_arr
+        val = val[(jnp.arange(n_axis) - local_part) % n_axis]
+        return _return_all_cycles(val, dimension_no)
+
     full_reassemble, full_merging, full_predict = (
         lax.all_gather(reassemble, ("section", "dp"), axis=2, tiled=True),
         lax.all_gather(merging, ("section", "dp"), axis=2, tiled=True),
-        lax.all_gather(predict, ("section", "dp"), axis=0, tiled=True),
+        arrange_ratios(predict, ("section", "dp"), dimension_no=0),
     )
     zero_nudges = jnp.zeros((3, token_rows, inner_width), jnp.bfloat16)
     zero_rows = jnp.zeros(tokens.shape[1:], jnp.float32)

time: 987 us -> 1040 us (1.054)
  waiting for transfers between devices: 475 us -> 529 us
  blocking collectives: 49.4 us -> 20.1 us
  starting transfers between devices: 56.4 us -> 84.3 us
    psum x2, waiting for transfers between devices: 75.9 us -> 126 us  [broadcast(): return lax.psum(kept, axis)]
    all_gather x1 -> x0, blocking collectives: 31.5 us -> none  [on_device(): lax.all_gather(predict, ('section', 'dp'), axis=0, tiled=True)]
    ppermute x0 -> x15, starting transfers between devices: none -> 28.1 us  [the longest x7 27.6 us: arrange_ratios(): lax.ppermute(t1[-1] if t1 else sheet, axis_name=mesh_name, perm=ledger)]
    ppermute x0 -> x15, waiting for transfers between devices: none -> 11.5 us  [the longest x8 10.4 us: arrange_ratios(): lax.ppermute(u1[-1] if u1 else sheet, axis_name=mesh_name, perm=block_list)]
    unnamed x43 -> x62, local copies, waits for them, and re-layouts: 85.7 us -> 86.9 us
  transfers between devices with their start and end apart: 24 -> 39, of which waited for: 20 -> 29; matrix products, arithmetic and copies ran while one was open for 20% -> 19% of each run, Pallas kernels for 0% -> 0%
where the time goes in v1:
time: 1040 us; the launch traced here: 1030 us
  waiting for transfers between devices  529 us (51%)
  matrix products  149 us (14%)
  local copies, waits for them, and re-layouts  143 us (14%)
  other arithmetic  88.3 us (8%)
  starting transfers between devices  84.3 us (8%)
  blocking collectives  20.1 us (2%)
  between operations  19.3 us (2%)
    psum x2, waiting for transfers between devices, broadcast(): return lax.psum(kept, axis)  126 us
    ppermute x14, waiting for transfers between devices, passed_along(): return lax.ppermute(block, axis, route)  104 us
    unnamed x14, waiting for transfers between devices  102 us
    reduce_scatter x1, waiting for transfers between devices, on_device(): lax.psum_scatter(grad_reassemble.astype(jnp.float32), ('section', 'dp'),...  90.2 us
    unnamed x62, local copies, waits for them, and re-layouts  86.9 us
    select_n x42, other arithmetic, put_slot(): return jnp.where(active, updated, store_array)  65.6 us
    reduce_scatter x1, waiting for transfers between devices, on_device(): lax.psum_scatter(grad_merging.astype(jnp.float32), ('section', 'dp'), sca...  58.5 us
    ppermute x14, starting transfers between devices, passed_along(): return lax.ppermute(block, axis, route)  55.4 us
  transfers between devices with their start and end apart: 39, of which 29 were waited for; matrix products, arithmetic and copies ran while one was open for 19% of the time, Pallas kernels for 0%

profile of v1, /device:TPU:0, one launch (start us, length us, event | category | flops | bytes accessed | tf_op | source)
XLA Modules:
  0.0 1034.8 jit_solution(6327592184322416767)
XLA Ops:
  7.7 6.5 collective-permute-done.2
  14.2 4.4 collective-permute-start.10
  20.2 4.4 collective-permute-start.11
  25.9 4.4 collective-permute-start.12
  32.2 4.4 collective-permute-start.13
  38.6 4.5 collective-permute-start.14
  44.3 4.4 collective-permute-start.15
  48.8 20.1 %all_gather.7 = bf16[4,128,128]{1,0,2:T(4,128)(2,1)} all-gather(bf16[4,128,8]{1,0,2:T(4,128)(2,1)S(1)} %copy.220), channel_id=1, replica_groups=mesh['group'=2,'section'=4,'dp'=4] {'section','dp'}, dimensions={2}, use_global_device_ids=true | all-gather | bytes 139264 | tf_op jit(solution)/shard_map/all_gather | solution.py:167
  73.1 4.3 copy.218
  77.3 5.3 copy.219
  82.6 5.3 copy.217
  90.7 124.5 %while.42 = (s32[]{:T(128)}, f32[1,32,1600]{2,1,0:T(8,128)S(1)}, f32[4,1,32,1600]{3,2,1,0:T(8,128)}, bf16[4,1,32,1600]{3,2,1,0:T(8,128)(2,1)}, s32[]{:T(128)}, /...) while((s32[]{:T(128)}, f32[1,32,1600]{2,1,0:T(8,128)S(1)}, ...), condition=%wide.region_6.7_spmd, body=%wide.region_0.6_spmd.sunk | while | flops 344828992 | bytes 25776712 | solution.py:194
  92.4 10.4 %conditional.7 = (f32[1,32,1600]{2,1,0:T(8,128)S(1)}) conditional(s32[]{:T(128)} %convert_element_type.926, f32[1,32,1600]{2,1,0:T(8,128)S(1)} %get-tuple-element.1335, (f32[1,32,1600]{2,1,0:T(8,128)S(1)}, bf16[1600,832]{1,0:T(8,128)(2,1)}, bf16[1600,832]{1,0:T(8,128)(2,1)S(1)}, bf16[1600,832]{1,0:T(8,128)(2,1)}, bf16[832,1600]{1,0:T(8,128)(2,1)}) %tuple.182), branch_computations={%region_1.1_spmd, %region_2.5_spmd} | conditional | flops 344624192 | bytes 23596836 | solution.py:188
  110.2 10.4 %conditional.7 = (f32[1,32,1600]{2,1,0:T(8,128)S(1)}) conditional(s32[]{:T(128)} %convert_element_type.926, f32[1,32,1600]{2,1,0:T(8,128)S(1)} %get-tuple-element.1335, (f32[1,32,1600]{2,1,0:T(8,128)S(1)}, bf16[1600,832]{1,0:T(8,128)(2,1)}, bf16[1600,832]{1,0:T(8,128)(2,1)S(1)}, bf16[1600,832]{1,0:T(8,128)(2,1)}, bf16[832,1600]{1,0:T(8,128)(2,1)}) %tuple.182), branch_computations={%region_1.1_spmd, %region_2.5_spmd} | conditional | flops 344624192 | bytes 23596836 | solution.py:188
  120.6 4.4 collective-permute-start
  130.2 10.4 %conditional.7 = (f32[1,32,1600]{2,1,0:T(8,128)S(1)}) conditional(s32[]{:T(128)} %convert_element_type.926, f32[1,32,1600]{2,1,0:T(8,128)S(1)} %get-tuple-element.1335, (f32[1,32,1600]{2,1,0:T(8,128)S(1)}, bf16[1600,832]{1,0:T(8,128)(2,1)}, bf16[1600,832]{1,0:T(8,128)(2,1)S(1)}, bf16[1600,832]{1,0:T(8,128)(2,1)}, bf16[832,1600]{1,0:T(8,128)(2,1)}) %tuple.182), branch_computations={%region_1.1_spmd, %region_2.5_spmd} | conditional | flops 344624192 | bytes 23596836 | solution.py:188
  140.6 4.4 collective-permute-start
  150.1 10.4 %conditional.7 = (f32[1,32,1600]{2,1,0:T(8,128)S(1)}) conditional(s32[]{:T(128)} %convert_element_type.926, f32[1,32,1600]{2,1,0:T(8,128)S(1)} %get-tuple-element.1335, (f32[1,32,1600]{2,1,0:T(8,128)S(1)}, bf16[1600,832]{1,0:T(8,128)(2,1)}, bf16[1600,832]{1,0:T(8,128)(2,1)S(1)}, bf16[1600,832]{1,0:T(8,128)(2,1)}, bf16[832,1600]{1,0:T(8,128)(2,1)}) %tuple.182), branch_computations={%region_1.1_spmd, %region_2.5_spmd} | conditional | flops 344624192 | bytes 23596836 | solution.py:188
  160.4 4.4 collective-permute-start
  169.9 14.8 %collective-permute-start = (f32[1,32,1600]{2,1,0:T(8,128)S(1)}, f32[1,32,1600]{2,1,0:T(8,128)S(1)}, u32[]{:S(2)}, u32[]{:S(2)}) collective-permute-start(f32[1,32,1600]{2,1,0:T(8,128)S(1)} %get-tuple-element.1488), channel_id=1, source_target_pairs={{0,4},{4,8},{8,12},{1,5},{5,9},{9,13},{2,6},{6,10},{10,14},{3,7},{... | collective-permute-start | bytes 614408 | tf_op jit(solution)/shard_map/while/body/eval_jaxpr/ppermute | solution.py:21
  189.7 4.4 collective-permute-start
  199.2 12.7 %collective-permute-start = (f32[1,32,1600]{2,1,0:T(8,128)S(1)}, f32[1,32,1600]{2,1,0:T(8,128)S(1)}, u32[]{:S(2)}, u32[]{:S(2)}) collective-permute-start(f32[1,32,1600]{2,1,0:T(8,128)S(1)} %get-tuple-element.1488), channel_id=1, source_target_pairs={{0,4},{4,8},{8,12},{1,5},{5,9},{9,13},{2,6},{6,10},{10,14},{3,7},{... | collective-permute-start | bytes 614408 | tf_op jit(solution)/shard_map/while/body/eval_jaxpr/ppermute | solution.py:21
  223.6 47.8 %all-reduce.13.cloned.1.call-done = (bf16[128,128]{1,0:T(8,128)(2,1)}, bf16[128,128]{1,0:T(8,128)(2,1)}, bf16[128,128]{1,0:T(8,128)(2,1)}, bf16[128,128]{1,0:T(8,128)(2,1)}) async-done(((bf16[128,128]{1,0:T(8,128)(2,1)}, bf16[128,128]{1,0:T(8,128)(2,1)}, bf16[128,128]{1,0:T(8,128)(2,1)}, bf16[128,128]{1,0:T(8,128)(2,1)}), (bf16[128,128]{1,0:T(8,128)(2,1)}, bf16[128,128]{1,0:T(8,128)(2,1)}, ...) | async-done | bytes 131088 | tf_op jit(solution)/shard_map/psum | solution.py:26
  271.4 4.9 conditional.3
  280.5 77.7 %all-reduce.11.cloned.1.call-done = bf16[4,128,128]{2,1,0:T(8,128)(2,1)} async-done(((bf16[4,128,128]{2,1,0:T(8,128)(2,1)}), bf16[4,128,128]{2,1,0:T(8,128)(2,1)}) %all-reduce.11.cloned.1.call-update) | async-done | bytes 131088 | tf_op jit(solution)/shard_map/psum | solution.py:26
  369.3 278.7 %while.43 = (s32[]{:T(128)}, f32[1,32,1600]{2,1,0:T(8,128)S(1)}, bf16[4,3,32,832]{3,2,0,1:T(8,128)(2,1)}, bf16[4,32,1600]{2,1,0:T(8,128)(2,1)}, bf16[4,32,832]{2...) while((s32[]{:T(128)}, f32[1,32,1600]{2,1,0:T(8,128)S(1)}, ...), condition=%wide.region_24.25_spmd.clone, body=%wide.region_16.24_spmd.clone.sunk | while | flops 608857152 | bytes 61259056 | solution.py:302
  398.4 87.2 %collective-permute-done.1 = bf16[1,32,1600]{2,1,0:T(8,128)(2,1)S(1)} collective-permute-done((bf16[1,32,1600]{2,1,0:T(8,128)(2,1)}, bf16[1,32,1600]{2,1,0:T(8,128)(2,1)S(1)}, u32[]{:S(2)}, u32[]{:S(2)}) %collective-permute-start.1) | collective-permute-done | bytes 102432 | tf_op jit(solution)/shard_map/while/body/eval_jaxpr/ppermute | solution.py:21
  487.4 31.3 %conditional.8 = (bf16[1,32,1600]{2,1,0:T(8,128)(2,1)}, bf16[1,3,32,832]{3,2,1,0:T(8,128)(2,1)S(1)}, bf16[1,32,1600]{2,1,0:T(8,128)(2,1)}, bf16[1,32,832]{2,1,0:T(8,128)(2,1)S(1)}) conditional(s32[]{:T(128)} %convert_element_type.927, () %tuple.185, (f32[1,32,1600]{2,1,0:T(8,128)S(1)}, bf16[832,1600]{1,0:T(8,128)(2,1)}, ...), branch_computations={%region_17.17_spmd, %region_18.23_spmd} | conditional | flops 608443456 | bytes 57541052 | solution.py:281
  512.0 2.9 convolution_convert_fusion.5
  528.2 31.3 %conditional.8 = (bf16[1,32,1600]{2,1,0:T(8,128)(2,1)}, bf16[1,3,32,832]{3,2,1,0:T(8,128)(2,1)S(1)}, bf16[1,32,1600]{2,1,0:T(8,128)(2,1)}, bf16[1,32,832]{2,1,0:T(8,128)(2,1)S(1)}) conditional(s32[]{:T(128)} %convert_element_type.927, () %tuple.185, (f32[1,32,1600]{2,1,0:T(8,128)S(1)}, bf16[832,1600]{1,0:T(8,128)(2,1)}, ...), branch_computations={%region_17.17_spmd, %region_18.23_spmd} | conditional | flops 608443456 | bytes 57541052 | solution.py:281
  568.9 31.3 %conditional.8 = (bf16[1,32,1600]{2,1,0:T(8,128)(2,1)}, bf16[1,3,32,832]{3,2,1,0:T(8,128)(2,1)S(1)}, bf16[1,32,1600]{2,1,0:T(8,128)(2,1)}, bf16[1,32,832]{2,1,0:T(8,128)(2,1)S(1)}) conditional(s32[]{:T(128)} %convert_element_type.927, () %tuple.185, (f32[1,32,1600]{2,1,0:T(8,128)S(1)}, bf16[832,1600]{1,0:T(8,128)(2,1)}, ...), branch_computations={%region_17.17_spmd, %region_18.23_spmd} | conditional | flops 608443456 | bytes 57541052 | solution.py:281
  593.4 2.9 convolution_convert_fusion.5
  609.7 31.3 %conditional.8 = (bf16[1,32,1600]{2,1,0:T(8,128)(2,1)}, bf16[1,3,32,832]{3,2,1,0:T(8,128)(2,1)S(1)}, bf16[1,32,1600]{2,1,0:T(8,128)(2,1)}, bf16[1,32,832]{2,1,0:T(8,128)(2,1)S(1)}) conditional(s32[]{:T(128)} %convert_element_type.927, () %tuple.185, (f32[1,32,1600]{2,1,0:T(8,128)S(1)}, bf16[832,1600]{1,0:T(8,128)(2,1)}, ...), branch_computations={%region_17.17_spmd, %region_18.23_spmd} | conditional | flops 608443456 | bytes 57541052 | solution.py:281
  634.2 2.9 convolution_convert_fusion.5
  650.0 12.4 %copy.245 = bf16[1,1600,832]{2,0,1:T(2,128)(2,1)} copy(bf16[1,1600,832]{1,2,0:T(8,128)(2,1)S(1)} %fusion.97) | data formatting | bytes 5324800
  662.4 4.7 copy.335
  670.8 14.5 %copy.247 = bf16[1,1600,832]{2,0,1:T(2,128)(2,1)} copy(bf16[1,1600,832]{1,2,0:T(8,128)(2,1)} %fusion.98) | data formatting | bytes 5324800
  685.3 4.7 copy.334
  692.7 14.3 %copy.243 = bf16[1,1600,832]{2,0,1:T(2,128)(2,1)} copy(bf16[1,1600,832]{1,2,0:T(8,128)(2,1)} %fusion.96) | data formatting | bytes 5324800
  707.0 4.6 copy.336
  718.2 4.8 copy.232
  726.6 3.4 fusion.95
  732.9 8.6 reduce-scatter.26.cloned.1.call-done
  744.3 35.8 %reduce-scatter.22.cloned.1.call-done = bf16[400,832]{1,0:T(8,128)(2,1)} async-done(((bf16[1600,832]{1,0:T(8,128)(2,1)}), bf16[400,832]{1,0:T(8,128)(2,1)}) %reduce-scatter.22.cloned.1.call-update) | async-done | bytes 665616
  783.0 90.2 %reduce-scatter.18.cloned.1.call-done = f32[5,1600,8]{1,0,2:T(8,128)} async-done(((f32[5,1600,128]{1,0,2:T(8,128)}), f32[5,1600,8]{1,0,2:T(8,128)}) %reduce-scatter.18.cloned.1.call-update) | async-done | bytes 256016 | tf_op jit(solution)/shard_map/reduce_scatter | solution.py:331
  874.9 56.8 %reduce-scatter.28.cloned.1.call-done = f32[8,196]{1,0:T(8,128)} async-done(((f32[128,196]{1,0:T(8,128)}), f32[8,196]{1,0:T(8,128)}) %reduce-scatter.28.cloned.1.call-update) | async-done | bytes 6288
  931.8 58.5 %reduce-scatter.20.cloned.1.call-done = f32[4,128,8]{1,2,0:T(8,128)} async-done(((f32[4,128,128]{1,2,0:T(8,128)}), f32[4,128,8]{1,2,0:T(8,128)}) %reduce-scatter.20.cloned.1.call-update) | async-done | bytes 16400 | tf_op jit(solution)/shard_map/reduce_scatter | solution.py:334
  990.3 37.6 %reduce-scatter.16.cloned.1.call-done = bf16[1,208,1600]{2,1,0:T(8,128)(2,1)} async-done(((bf16[1,832,1600]{2,1,0:T(8,128)(2,1)}), bf16[1,208,1600]{2,1,0:T(8,128)(2,1)}) %reduce-scatter.16.cloned.1.call-update) | async-done | bytes 665616 | tf_op jit(solution)/shard_map/reduce_scatter | solution.py:326
  (490 shorter events, 332.3 us)
Async XLA Ops:
  7.2 208.1 %all-gather.2.cloned.1.call-start = ((), (), s32[]{:S(2)}) async-start(), calls=%async_computation.7 | async-start | bytes 2263040 | tf_op jit(solution)/shard_map/all_gather | solution.py:166
  7.2 7.0 collective-permute-start.2
  14.2 5.7 collective-permute-start.3
  14.2 6.0 collective-permute-start.10
  19.9 5.7 collective-permute-start.4
  20.2 5.7 collective-permute-start.11
  25.6 5.7 collective-permute-start.5
  25.7 245.7 %all-reduce.13.cloned.1.call-start = ((), (), s32[]{:S(2)}) async-start(), calls=%async_computation.16 | async-start | bytes 262144 | tf_op jit(solution)/shard_map/psum | solution.py:26
  25.9 6.3 collective-permute-start.12
  31.4 5.7 collective-permute-start.6
  32.2 6.4 collective-permute-start.13
  37.1 5.9 collective-permute-start.7
  38.6 5.8 collective-permute-start.14
  43.0 5.7 collective-permute-start.8
  44.3 43.5 %collective-permute-start.15 = (bf16[8,196]{1,0:T(8,128)(2,1)S(1)}, bf16[8,196]{1,0:T(8,128)(2,1)S(1)}, u32[]{:S(2)}, u32[]{:S(2)}) collective-permute-start(bf16[8,196]{1,0:T(8,128)(2,1)S(1)} %collective-permute-done.14), channel_id=1, source_target_pairs={{1,0},{2,1},{3,2},{4,3},{5,4},{6,5},{7,6},{8,7},{9,8},{10,9},{11,1... | collective-permute-start | bytes 9416 | tf_op jit(solution)/shard_map/ppermute | solution.py:155
  48.8 40.1 %collective-permute-start.9 = (bf16[8,196]{1,0:T(8,128)(2,1)S(1)}, bf16[8,196]{1,0:T(8,128)(2,1)S(1)}, u32[]{:S(2)}, u32[]{:S(2)}) collective-permute-start(bf16[8,196]{1,0:T(8,128)(2,1)S(1)} %collective-permute-done.8), channel_id=1, source_target_pairs={{0,1},{1,2},{2,3},{3,4},{4,5},{5,6},{6,7},{7,8},{8,9},{9,10},{10,1... | collective-permute-start | bytes 9416 | tf_op jit(solution)/shard_map/ppermute | solution.py:150
  82.6 6.4 copy-start.20
  87.9 135.7 %collective-permute-start.16 = (bf16[8,196]{1,0:T(8,128)(2,1)S(1)}, bf16[8,196]{1,0:T(8,128)(2,1)S(1)}, u32[]{:S(2)}, u32[]{:S(2)}) collective-permute-start(bf16[8,196]{1,0:T(8,128)(2,1)S(1)} %collective-permute-done.15), channel_id=1, source_target_pairs={{1,0},{2,1},{3,2},{4,3},{5,4},{6,5},{7,6},{8,7},{9,8},{10,9},{11,1... | collective-permute-start | bytes 9416 | tf_op jit(solution)/shard_map/ppermute | solution.py:155
  102.8 5.7 collective-permute-start
  120.6 7.9 collective-permute-start
  140.6 7.8 collective-permute-start
  160.4 7.7 collective-permute-start
  169.9 18.1 %collective-permute-start = (f32[1,32,1600]{2,1,0:T(8,128)S(1)}, f32[1,32,1600]{2,1,0:T(8,128)S(1)}, u32[]{:S(2)}, u32[]{:S(2)}) collective-permute-start(f32[1,32,1600]{2,1,0:T(8,128)S(1)} %get-tuple-element.1488), channel_id=1, source_target_pairs={{0,4},{4,8},{8,12},{1,5},{5,9},{9,13},{2,6},{6,10},{10,14},{3,7},{... | collective-permute-start | bytes 614408 | tf_op jit(solution)/shard_map/while/body/eval_jaxpr/ppermute | solution.py:21
  189.7 7.7 collective-permute-start
  199.2 16.0 %collective-permute-start = (f32[1,32,1600]{2,1,0:T(8,128)S(1)}, f32[1,32,1600]{2,1,0:T(8,128)S(1)}, u32[]{:S(2)}, u32[]{:S(2)}) collective-permute-start(f32[1,32,1600]{2,1,0:T(8,128)S(1)} %get-tuple-element.1488), channel_id=1, source_target_pairs={{0,4},{4,8},{8,12},{1,5},{5,9},{9,13},{2,6},{6,10},{10,14},{3,7},{... | collective-permute-start | bytes 614408 | tf_op jit(solution)/shard_map/while/body/eval_jaxpr/ppermute | solution.py:21
  215.2 8.4 copy-start.16
  215.2 56.2 %copy-start.12 = (bf16[4,128,128]{1,0,2:T(4,128)(2,1)S(1)}, bf16[4,128,128]{1,0,2:T(4,128)(2,1)}, u32[]{:S(2)}) copy-start(bf16[4,128,128]{1,0,2:T(4,128)(2,1)} %all_gather.7) | copy-start | bytes 393220
  215.2 56.2 %copy-start.17 = (s32[4,1,384]{2,1,0:T(1,128)S(1)}, s32[4,1,384]{2,1,0:T(1,128)}, u32[]{:S(2)}) copy-start(s32[4,1,384]{2,1,0:T(1,128)} %param.23) | copy-start | bytes 18436
  215.2 56.2 %copy-start.18 = (s32[4,1,384]{2,1,0:T(1,128)S(1)}, s32[4,1,384]{2,1,0:T(1,128)}, u32[]{:S(2)}) copy-start(s32[4,1,384]{2,1,0:T(1,128)} %param.24) | copy-start | bytes 18436
  215.2 56.2 %copy-start.19 = (f32[4,1,384]{2,1,0:T(1,128)S(1)}, f32[4,1,384]{2,1,0:T(1,128)}, u32[]{:S(2)}) copy-start(f32[4,1,384]{2,1,0:T(1,128)} %param.25) | copy-start | bytes 18436
  223.5 134.7 %all-reduce.11.cloned.1.call-start = ((), (), s32[]{:S(2)}) async-start(), calls=%async_computation.8 | async-start | bytes 262144 | tf_op jit(solution)/shard_map/psum | solution.py:26
  277.9 452.2 %reduce-scatter.24.cloned.1.call-start = ((), (), s32[]{:S(2)}) async-start(), calls=%async_computation.13 | async-start | bytes 3584000
  372.4 6.8 collective-permute-start.1
  382.4 6.8 collective-permute-start.1
  392.4 93.2 %collective-permute-start.1 = (bf16[1,32,1600]{2,1,0:T(8,128)(2,1)}, bf16[1,32,1600]{2,1,0:T(8,128)(2,1)S(1)}, u32[]{:S(2)}, u32[]{:S(2)}) collective-permute-start(bf16[1,32,1600]{2,1,0:T(8,128)(2,1)} %get-tuple-element.1353), channel_id=1, source_target_pairs={{4,0},{8,4},{12,8},{5,1},{9,5},{13,9},{6,2},{10,6},{14,10},{7,3},{... | collective-permute-start | bytes 307208 | tf_op jit(solution)/shard_map/while/body/eval_jaxpr/ppermute | solution.py:21
  514.9 3.8 copy-start.7
  518.7 7.6 collective-permute-start.1
  555.6 3.8 copy-start.7
  559.5 7.6 collective-permute-start.1
  600.2 7.6 collective-permute-start.1
  641.0 7.0 collective-permute-start.1
  667.1 74.5 %reduce-scatter.26.cloned.1.call-start = ((), (), s32[]{:S(2)}) async-start(), calls=%async_computation.14 | async-start | bytes 3584000
  690.0 90.2 %reduce-scatter.22.cloned.1.call-start = ((), (), s32[]{:S(2)}) async-start(), calls=%async_computation.12 | async-start | bytes 3584000
  711.6 6.5 copy-start.11
  711.7 161.5 %reduce-scatter.18.cloned.1.call-start = ((), (), s32[]{:S(2)}) async-start(), calls=%async_computation.10 | async-start | bytes 7241728 | tf_op jit(solution)/shard_map/reduce_scatter | solution.py:331
  723.1 208.7 %reduce-scatter.28.cloned.1.call-start = ((), (), s32[]{:S(2)}) async-start(), calls=%async_computation.15 | async-start | bytes 139264
  724.7 265.5 %reduce-scatter.20.cloned.1.call-start = ((), (), s32[]{:S(2)}) async-start(), calls=%async_computation.11 | async-start | bytes 278528 | tf_op jit(solution)/shard_map/reduce_scatter | solution.py:334
  726.6 301.4 %reduce-scatter.16.cloned.1.call-start = ((), (), s32[]{:S(2)}) async-start(), calls=%async_computation.9 | async-start | bytes 3461120 | tf_op jit(solution)/shard_map/reduce_scatter | solution.py:326
  (36 other events, 97.2 us)
Sparse Core Ops, SparseCore 0:
  25.8 43.5 all-gather.1
  223.6 47.7 all-reduce.12
  278.0 80.1 all-reduce.10
  667.2 35.4 reduce-scatter.23
  705.3 36.2 reduce-scatter.25
  743.9 36.2 reduce-scatter.21
  784.7 88.4 reduce-scatter.17
  877.2 54.5 reduce-scatter.27
  935.9 54.3 reduce-scatter.19
  993.3 34.6 reduce-scatter.15
